TPU v7x, 128 devices: a whole 4x4x4 slice. The times are simulated.
128 devices in a mesh: row: 8 (over z, x_lo), col: 16 (over x_hi, y, core).
Axes of the slice: x: 4 (x_hi: 2, x_lo: 2; x = x_hi * 2 + x_lo), y: 4, z: 4, core: 2. Of those that a mesh axis runs over, the one named last changes fastest.
Arguments:
- front: float32 [45056, 4096], P('row', 'col'), may hold values from -6 to 278, as said below
- children: float32 [32768, 4096], P('row', 'col'), may hold values from -6 to 6
- row_map: int32 [256], replicated, may hold values from 0 to 351, as said below
- col_map: int32 [64], replicated, may hold values from 0 to 31, as said below
Outputs:
- updated: float32 [45056, 4096], P('row', 'col')
Inputs may be any that keep to these rules, and one draw needn't show every extreme that they name: `front`: the symmetric part of the assembled leading 512 x 512 block is positive definite. `row_map`: within one child no front row block is named twice. Of the 32 child row blocks stored on one device, at most 8 name front row blocks of one owner (block index modulo 8); one owner, the same for every device, is named exactly 8 times by every device. Within one child no front column block is named twice, and col_map[h * 32 + b] modulo 16 equals b // 2.
All inputs are finite; a program needn't handle non-finite values.
Results may differ from a plain program's by a relative error of at most 0.00005.
Values sent between devices are 32-bit elements; how exact they have to be, the bound alone decides.
A program may use at most 128 MiB of HBM per device.

v0:
```python
import jax
import jax.numpy as jnp
from jax import lax
from jax.sharding import PartitionSpec as P

BLK = 128
PANEL = 512


def broadcast(x, axis, root):
    mine = lax.axis_index(axis) == root
    return lax.psum(jnp.where(mine, x, jnp.zeros_like(x)), axis)


def factor_rows(panel_rows, lower_factor):
    return jax.scipy.linalg.solve_triangular(lower_factor, panel_rows.T, lower=True).T


def local(front, children, row_map, col_map):
    row_count = lax.axis_size("row")
    col_count = lax.axis_size("col")
    my_row = lax.axis_index("row")
    my_col = lax.axis_index("col")
    local_rows = front.shape[0] // BLK
    local_cols = front.shape[1] // BLK
    child_rows = children.shape[0] // BLK
    child_cols = children.shape[1] // BLK
    halfway = row_count // 2
    capacity = 2 * child_rows // row_count
    slot_count = row_count * capacity
    layout = row_map.reshape(row_count, child_rows)
    owner_rows = layout % row_count
    local_place = layout // row_count
    counter = jnp.arange(child_rows)
    earlier = (owner_rows[:, :, None] == owner_rows[:, None, :]) & (
        counter[None, None, :] < counter[None, :, None]
    )
    rank_index = jnp.sum(earlier.astype(jnp.int32), axis=2)
    slot_index = owner_rows * capacity + rank_index
    my_slots = lax.dynamic_index_in_dim(slot_index, my_row, 0, keepdims=False)
    picker = (jnp.arange(slot_count)[:, None] == my_slots[None, :]).astype(jnp.float32)
    flat_rows = children.reshape(child_rows, BLK * child_cols * BLK)
    outgoing = jnp.dot(picker, flat_rows, precision=lax.Precision.HIGHEST).reshape(
        row_count, capacity, BLK * child_cols * BLK
    )
    incoming = lax.all_to_all(outgoing, "row", split_axis=0, concat_axis=0, tiled=True)
    is_mine = owner_rows == my_row
    slot_of = jnp.where(is_mine, rank_index, -1)
    slot_hit = (slot_of[:, :, None] == jnp.arange(capacity)[None, None, :]).astype(jnp.float32)
    target = (local_place[:, :, None] == jnp.arange(local_rows)[None, None, :]).astype(jnp.float32)
    row_route = jnp.einsum(
        "sum,suk->ksm", slot_hit, target, precision=lax.Precision.HIGHEST
    ).reshape(local_rows, slot_count)
    column_maps = col_map.reshape(2, col_count, child_cols)
    my_columns = lax.dynamic_index_in_dim(column_maps, my_col, 1, keepdims=False) // col_count
    source_columns = my_columns[jnp.arange(row_count) // halfway]
    column_pick = (source_columns[:, :, None] == jnp.arange(local_cols)[None, None, :]).astype(
        jnp.float32
    )
    received = incoming.reshape(row_count, capacity, BLK, child_cols, BLK)
    placed = jnp.einsum("stq,smitj->smiqj", column_pick, received, precision=lax.Precision.HIGHEST)
    placed = placed.reshape(slot_count, BLK * local_cols * BLK)
    added_tiles = jnp.dot(row_route, placed, precision=lax.Precision.HIGHEST).reshape(
        local_rows * BLK, local_cols * BLK
    )
    assembled = front + added_tiles
    panel_blocks = PANEL // BLK
    own_block = assembled[:, :BLK]
    pieces = []
    for source in range(panel_blocks):
        pieces.append(broadcast(own_block, "col", source))
    panel_block = jnp.concatenate(pieces, axis=1)
    leading = lax.all_gather(panel_block[:BLK], "row", axis=0, tiled=True)[:PANEL]
    lower_factor = jnp.linalg.cholesky((leading + leading.T) * 0.5)
    factor = factor_rows(panel_block, lower_factor)
    lead_rows = lax.dynamic_slice_in_dim(
        lower_factor, jnp.minimum(my_row, panel_blocks - 1) * BLK, BLK, 0
    )
    first_rows = jnp.where(my_row < panel_blocks, lead_rows, factor[:BLK])
    factor = jnp.concatenate([first_rows, factor[BLK:]], axis=0)
    stride = col_count // row_count
    wanted = jnp.arange(local_cols) * stride + my_col // row_count
    chosen = factor.reshape(local_rows, BLK, PANEL)[wanted].reshape(local_cols * BLK, PANEL)
    across = broadcast(chosen, "row", my_col % row_count)
    trailing = assembled - jnp.dot(factor, across.T, precision=lax.Precision.HIGHEST)
    panel_col = lax.dynamic_slice_in_dim(
        factor, jnp.minimum(my_col, panel_blocks - 1) * BLK, BLK, 1
    )
    first_cols = jnp.where(my_col < panel_blocks, panel_col, trailing[:, :BLK])
    return jnp.concatenate([first_cols, trailing[:, BLK:]], axis=1)


def solution(mesh):
    placed = (P("row", "col"), P("row", "col"), P(), P())
    return jax.shard_map(
        local, mesh=mesh, in_specs=placed, out_specs=P("row", "col"), check_vma=False
    )
```

profile of v0, /device:TPU:0, one launch (start us, length us, event | category | flops | bytes accessed | tf_op | source)
XLA Modules:
  0.0 753.7 jit_solution(13739279627590797800)
XLA Ops:
  7.6 4.9 reshape.288
  12.6 8.4 %fusion.42 = f32[8,8,32768]{2,1,0:T(8,128)} fusion(f32[32,32768,1]{1,0,2:T(8,128)} %reshape.288, s32[32]{0:T(128)S(1)} %fusion.54, s32[8,8]{1,0:T(8,128)S(1)} %multiply_add_fusion.1), kind=kOutput, calls=%fused_computation.82 | convolution fusion | flops 805308416 | bytes 12583296 | tf_op jit(solution)/shard_map/dot_general | solution.py:43
  21.0 6.5 all-to-all-start
  28.2 6.2 copy.34
  35.2 86.8 %all-to-all-done = f32[8,8,32768]{2,1,0:T(8,128)} async-done(((f32[8,8,32768]{2,1,0:T(8,128)}), f32[8,8,32768]{2,1,0:T(8,128)}, u32[]{:S(2)}, u32[]{:S(2)}) %all-to-all-start) | async-done | bytes 8388640 | tf_op jit(solution)/shard_map/all_to_all | solution.py:46
  122.0 23.5 %fusion.14 = f32[8,8,128,2,128]{4,3,2,1,0:T(2,128)} fusion(f32[8,8,128,2,128]{4,1,3,2,0:T(8,128)} %bitcast.3, s32[8,2]{1,0:T(8,128)S(1)} %gather_fusion), kind=kOutput, calls=%fused_computation.24 | convolution fusion | flops 50331680 | bytes 16777280 | tf_op jit(solution)/shard_map/stq,smitj->smiqj/dot_general | solution.py:61
  145.5 11.5 %reshape.250 = f32[64,32768]{1,0:T(8,128)} reshape(f32[8,8,128,2,128]{4,3,2,1,0:T(2,128)} %fusion.14) | data formatting | bytes 16777216 | tf_op jit(solution)/shard_map/reshape | solution.py:62
  157.0 10.1 %fusion.59 = f32[44,32768]{1,0:T(8,128)} fusion(f32[44,64]{0,1:T(8,128)S(1)} %convolution_bitcast_fusion, f32[64,32768]{1,0:T(8,128)} %reshape.250), kind=kOutput, calls=%fused_computation.136 | convolution fusion | flops 1107296256 | bytes 14167040 | tf_op jit(solution)/shard_map/dot_general | solution.py:63
  167.1 7.0 reshape.251
  174.1 6.3 copy.35
  180.4 5.0 add.152
  185.4 5.3 slice_select_fusion
  191.4 174.2 %all-reduce.7.cloned.1.call-done = (f32[5632,128]{0,1:T(8,128)}, f32[5632,128]{0,1:T(8,128)}, f32[5632,128]{0,1:T(8,128)}, f32[5632,128]{0,1:T(8,128)}) async-done(((f32[5632,128]{0,1:T(8,128)}, f32[5632,128]{0,1:T(8,128)}, f32[5632,128]{0,1:T(8,128)}, f32[5632,128]{0,1:T(8,128)}), (f32[5632,128]{0,1:T(8,128)}, f32[5632,128]{0,1:T(8,128)}, f32[5632,128]{0,1:T(8,128)}, ...) | async-done | bytes 11534352 | tf_op jit(solution)/shard_map/psum | solution.py:12
  365.7 2.2 constant_dynamic-update-slice_fusion.3
  370.6 4.3 copy-done.1
  376.0 51.0 %all-gather.2.cloned.1.call-done = f32[1024,512]{0,1:T(8,128)} async-done(((f32[128,512]{0,1:T(8,128)}), f32[1024,512]{0,1:T(8,128)}) %all-gather.2.cloned.1.call-update) | async-done | bytes 2097168 | tf_op jit(solution)/shard_map/all_gather | solution.py:73
  428.6 1.4 fusion.22
  430.6 11.7 %cholesky.104 = f32[128,128]{1,0:T(8,128)S(1)} custom-call(f32[128,128]{1,0:T(8,128)S(1)} %cholesky.266), custom_call_target="Cholesky" | custom-call | tf_op jit(solution)/shard_map/jit(cholesky)/cholesky | solution.py:74
  442.4 9.8 %custom-call.31 = f32[1,128,128]{1,2,0:T(8,128)S(1)} custom-call(f32[1,128,128]{2,1,0:T(8,128)S(1)} %get-tuple-element.52), custom_call_target="InvertDiagBlocksLowerTriangular" | custom-call | tf_op jit(solution)/shard_map/jit(cholesky)/cholesky | solution.py:74
  452.9 11.7 %cholesky.217 = f32[128,128]{1,0:T(8,128)S(1)} custom-call(f32[128,128]{1,0:T(8,128)S(1)} %cholesky.270), custom_call_target="Cholesky" | custom-call | tf_op jit(solution)/shard_map/jit(cholesky)/cholesky | solution.py:74
  465.0 10.2 %custom-call.32 = f32[1,128,128]{1,2,0:T(8,128)S(1)} custom-call(f32[1,128,128]{2,1,0:T(8,128)S(1)} %get-tuple-element.50), custom_call_target="InvertDiagBlocksLowerTriangular" | custom-call | tf_op jit(solution)/shard_map/jit(cholesky)/cholesky | solution.py:74
  476.2 11.7 %cholesky.238 = f32[128,128]{1,0:T(8,128)S(1)} custom-call(f32[128,128]{1,0:T(8,128)S(1)} %cholesky.275), custom_call_target="Cholesky" | custom-call | tf_op jit(solution)/shard_map/jit(cholesky)/cholesky | solution.py:74
  488.1 9.8 %custom-call.33 = f32[1,128,128]{1,2,0:T(8,128)S(1)} custom-call(f32[1,128,128]{2,1,0:T(8,128)S(1)} %get-tuple-element.48), custom_call_target="InvertDiagBlocksLowerTriangular" | custom-call | tf_op jit(solution)/shard_map/jit(cholesky)/cholesky | solution.py:74
  498.7 11.9 %cholesky.255 = f32[128,128]{1,0:T(8,128)S(1)} custom-call(f32[128,128]{1,0:T(8,128)S(1)} %convolution_subtract_fusion.5), custom_call_target="Cholesky" | custom-call | tf_op jit(solution)/shard_map/jit(cholesky)/cholesky | solution.py:74
  515.3 1.7 fusion.23
  517.0 15.1 %while.1 = (s32[]{:T(128)}, f32[512,512]{0,1:T(8,128)}, s32[4,2]{0,1:T(2,128)S(1)}, f32[4,128,128]{2,1,0:T(8,128)}, s32[]{:T(128)}) while((s32[]{:T(128)}, f32[512,512]{0,1:T(8,128)}, s32[4,2]{0,1:T(2,128)S(1)}, f32[4,128,128]{2,1,0:T(8,128)}, s32[]{:T(128)}) %tuple.33), condition=%wide.while_cond, body=%wide.while_body.sunk | while | flops 2 | bytes 393829 | solution.py:16
  517.7 2.6 dynamic-slice.7
  521.7 2.3 dynamic-slice.7
  525.4 2.3 dynamic-slice.7
  529.1 2.3 dynamic-slice.7
  532.1 40.1 %custom-call.34 = f32[4,128,128]{1,2,0:T(8,128)S(1)} custom-call(f32[4,128,128]{2,1,0:T(8,128)} %get-tuple-element.12), custom_call_target="InvertDiagBlocksLowerTriangular" | custom-call | tf_op jit(solution)/shard_map/jit(_solve_triangular)/triangular_solve | solution.py:16
  572.2 4.6 fusion.19
  576.9 4.8 convolution_subtract_fusion.1
  581.7 2.7 fusion.35
  584.5 4.5 convolution_subtract_fusion.2
  589.0 3.0 fusion.33
  592.0 7.0 fusion.8
  599.0 2.7 fusion.32
  601.8 4.6 maximum_bitcast_fusion
  606.4 9.1 %slice.161 = f32[5504,512]{0,1:T(8,128)} slice(f32[5632,512]{0,1:T(8,128)} %maximum_bitcast_fusion), slice={[128:5632], [0:512]} | slice | bytes 22544384 | tf_op jit(solution)/shard_map/slice | solution.py:80
  616.5 9.3 %pad_maximum_fusion = f32[5632,512]{0,1:T(8,128)} fusion(f32[128,512]{0,1:T(8,128)S(1)} %slice_select_fusion.4, f32[5504,512]{0,1:T(8,128)} %slice.161), kind=kLoop, calls=%fused_computation.5 | loop fusion | flops 2883584 | bytes 23068672 | tf_op jit(solution)/shard_map/concatenate | solution.py:80
  625.8 12.2 %copy.46 = f32[5632,512]{1,0:T(8,128)} copy(f32[5632,512]{0,1:T(8,128)} %pad_maximum_fusion) | data formatting | bytes 23068672 | tf_op jit(solution)/shard_map/concatenate | solution.py:80
  638.1 4.9 gather_fusion.1
  643.8 76.8 %all-reduce.5.cloned.1.call-done = f32[256,512]{1,0:T(8,128)} async-done(((f32[256,512]{1,0:T(8,128)}), f32[256,512]{1,0:T(8,128)}) %all-reduce.5.cloned.1.call-update) | async-done | bytes 524304 | tf_op jit(solution)/shard_map/psum | solution.py:12
  720.7 14.7 %convolution_subtract_fusion = f32[5632,256]{0,1:T(8,128)S(1)} fusion(f32[5632,256]{0,1:T(8,128)} %copy-done, f32[256,512]{1,0:T(8,128)} %all-reduce.5.cloned.1.call-done, f32[128,512]{0,1:T(8,128)S(1)} %slice_select_fusion.4, f32[5504,512]{0,1:T(8,128)} %slice.161), kind=kOutput, calls=%fused_computation.16 | convolution fusion | flops 8862695424 | bytes 23592960 | tf_op jit(solution)/shard_map/dot_general | solution.py:85
  735.4 2.3 fusion.18
  737.7 2.9 pad_maximum_fusion.1
  740.6 6.2 copy.47
  (95 shorter events, 21.9 us)
Async XLA Ops:
  21.0 7.0 copy-start.5
  21.0 101.0 %all-to-all-start = ((f32[8,8,32768]{2,1,0:T(8,128)}), f32[8,8,32768]{2,1,0:T(8,128)}, u32[]{:S(2)}, u32[]{:S(2)}) async-start(f32[8,8,32768]{2,1,0:T(8,128)} %fusion.42), calls=%async_computation | async-start | bytes 16777216 | tf_op jit(solution)/shard_map/all_to_all | solution.py:46
  27.5 338.2 %all-reduce.7.cloned.1.call-start = ((), (), s32[]{:S(2)}) async-start(), calls=%async_computation.3 | async-start | bytes 23068672 | tf_op jit(solution)/shard_map/psum | solution.py:12
  185.4 6.0 copy-start
  191.4 235.6 %all-gather.2.cloned.1.call-start = ((), (), s32[]{:S(2)}) async-start(), calls=%async_computation.1 | async-start | bytes 2359296 | tf_op jit(solution)/shard_map/all_gather | solution.py:73
  365.7 2.7 copy-start.4
  365.7 3.6 copy-start.3
  368.4 2.0 copy-start.2
  370.6 4.4 copy-start.1
  375.7 344.9 %all-reduce.5.cloned.1.call-start = ((), (), s32[]{:S(2)}) async-start(), calls=%async_computation.2 | async-start | bytes 1048576 | tf_op jit(solution)/shard_map/psum | solution.py:12
  517.0 67.5 %slice-start = ((s8[11534336]{0:T(1024)(128)(4,1)}), s8[3145728]{0:T(1024)(128)(4,1)S(1)}, s32[]{:S(2)}) async-start(s8[11534336]{0:T(1024)(128)(4,1)} %bitcast.80), calls=%async_computation.4 | async-start | bytes 6291456
  572.2 12.2 %slice-start.1 = ((s8[11534336]{0:T(1024)(128)(4,1)}), s8[4194304]{0:T(1024)(128)(4,1)S(1)}, s32[]{:S(2)}) async-start(s8[11534336]{0:T(1024)(128)(4,1)} %bitcast.80), calls=%async_computation.5 | async-start | bytes 8388608
  576.9 7.6 %slice-start.2 = ((s8[11534336]{0:T(1024)(128)(4,1)}), s8[4194304]{0:T(1024)(128)(4,1)S(1)}, s32[]{:S(2)}) async-start(s8[11534336]{0:T(1024)(128)(4,1)} %bitcast.80), calls=%async_computation.6 | async-start | bytes 8388608
Sparse Core Ops, SparseCore 0:
  191.5 174.1 all-reduce.6
  375.8 51.0 all-gather.1
  643.9 76.6 all-reduce.4
where the time goes:
time: 758 us; the launch traced here: 754 us
  waiting for transfers between devices  389 us (51%)
  other arithmetic  154 us (20%)
  local copies, waits for them, and re-layouts  98.2 us (13%)
  matrix products  88.7 us (12%)
  between operations  16.6 us (2%)
    psum x2, waiting for transfers between devices, broadcast(): return lax.psum(jnp.where(mine, x, jnp.zeros_like(x)), axis)  251 us
    all_to_all x1, waiting for transfers between devices, local(): lax.all_to_all(outgoing, 'row', split_axis=0, concat_axis=0, tiled=True)  86.8 us
    another operation x14, other arithmetic, local(): lower_factor = jnp.linalg.cholesky((leading + leading.T) * 0.5)  79 us
    all_gather x1, waiting for transfers between devices, local(): lax.all_gather(panel_block[:BLK], 'row', axis=0, tiled=True)[:PANEL]  51 us
    another operation x3, other arithmetic, factor_rows(): jax.scipy.linalg.solve_triangular(lower_factor, panel_rows.T, lower=True)  41.8 us
    another operation x7, matrix products, factor_rows(): jax.scipy.linalg.solve_triangular(lower_factor, panel_rows.T, lower=True)  29.4 us
    dot_general x1, matrix products, local(): jnp.einsum('stq,smitj->smiqj', column_pick, received, precision=lax.Preci...  23.5 us
    unnamed x22, local copies, waits for them, and re-layouts  16 us
  transfers between devices with their start and end apart: 4, of which 4 were waited for; matrix products, arithmetic and copies ran while one was open for 1% of the time, Pallas kernels for 0%

commit v1 on v0

--- a/solution.py
+++ b/solution.py
@@ -70,7 +70,9 @@
     for source in range(panel_blocks):
         pieces.append(broadcast(own_block, "col", source))
     panel_block = jnp.concatenate(pieces, axis=1)
-    leading = lax.all_gather(panel_block[:BLK], "row", axis=0, tiled=True)[:PANEL]
+    leading = jnp.concatenate(
+        lax.all_to_all(jnp.stack([panel_block[:BLK]] * lax.axis_size("row")), "row", 0, 0), axis=0
+    )[:PANEL]
     lower_factor = jnp.linalg.cholesky((leading + leading.T) * 0.5)
     factor = factor_rows(panel_block, lower_factor)
     lead_rows = lax.dynamic_slice_in_dim(

time: 758 us -> 732 us (0.966)
  waiting for transfers between devices: 389 us -> 365 us
  local copies, waits for them, and re-layouts: 98.2 us -> 74.9 us
  matrix products: 88.7 us -> 109 us
    all_gather x1 -> x0, waiting for transfers between devices: 51 us -> none  [local(): lax.all_gather(panel_block[:BLK], 'row', axis=0, tiled=True)[:PANEL]]
    all_to_all x0 -> x1, waiting for transfers between devices: none -> 24.6 us  [local(): lax.all_to_all(jnp.stack([panel_block[:BLK]] * lax.axis_size('row')), 'ro...]
    another operation x7, matrix products: 29.4 us -> 51.4 us  [factor_rows(): jax.scipy.linalg.solve_triangular(lower_factor, panel_rows.T, lower=True)]
    concatenate x2 -> x0, local copies, waits for them, and re-layouts: 18.5 us -> none  [the longest x1 12.2 us: local(): factor = jnp.concatenate([first_rows, factor[BLK:]], axis=0)]
    another operation x1 -> x4, local copies, waits for them, and re-layouts: 0.01 us -> 8.98 us  [factor_rows(): jax.scipy.linalg.solve_triangular(lower_factor, panel_rows.T, lower=True)]
    unnamed x22 -> x29, local copies, waits for them, and re-layouts: 16 us -> 15.1 us
  transfers between devices with their start and end apart: 4 -> 4, of which waited for: 4 -> 4; matrix products, arithmetic and copies ran while one was open for 1% -> 0% of each run, Pallas kernels for 0% -> 0%
where the time goes in v1:
time: 732 us; the launch traced here: 728 us
  waiting for transfers between devices  365 us (50%)
  other arithmetic  151 us (21%)
  matrix products  109 us (15%)
  local copies, waits for them, and re-layouts  74.9 us (10%)
  between operations  16.6 us (2%)
  starting transfers between devices  11.1 us (2%)
    psum x2, waiting for transfers between devices, broadcast(): return lax.psum(jnp.where(mine, x, jnp.zeros_like(x)), axis)  248 us
    all_to_all x1, waiting for transfers between devices, local(): lax.all_to_all(outgoing, 'row', split_axis=0, concat_axis=0, tiled=True)  93.3 us
    another operation x14, other arithmetic, local(): lower_factor = jnp.linalg.cholesky((leading + leading.T) * 0.5)  78.9 us
    another operation x7, matrix products, factor_rows(): jax.scipy.linalg.solve_triangular(lower_factor, panel_rows.T, lower=True)  51.4 us
    another operation x3, other arithmetic, factor_rows(): jax.scipy.linalg.solve_triangular(lower_factor, panel_rows.T, lower=True)  40.6 us
    all_to_all x1, waiting for transfers between devices, local(): lax.all_to_all(jnp.stack([panel_block[:BLK]] * lax.axis_size('row')), 'ro...  24.6 us
    dot_general x1, matrix products, local(): jnp.einsum('stq,smitj->smiqj', column_pick, received, precision=lax.Preci...  23.5 us
    unnamed x29, local copies, waits for them, and re-layouts  15.1 us
  transfers between devices with their start and end apart: 4, of which 4 were waited for; matrix products, arithmetic and copies ran while one was open for 0% of the time, Pallas kernels for 0%

profile of v1, /device:TPU:0, one launch (start us, length us, event | category | flops | bytes accessed | tf_op | source)
XLA Modules:
  0.0 728.4 jit_solution(4388328227401443523)
XLA Ops:
  7.6 4.9 reshape.292
  12.6 8.4 %fusion.42 = f32[8,8,32768]{2,1,0:T(8,128)} fusion(f32[32,32768,1]{1,0,2:T(8,128)} %reshape.292, s32[32]{0:T(128)S(1)} %fusion.54, s32[8,8]{1,0:T(8,128)S(1)} %multiply_add_fusion.1), kind=kOutput, calls=%fused_computation.84 | convolution fusion | flops 805308416 | bytes 12583296 | tf_op jit(solution)/shard_map/dot_general | solution.py:43
  21.0 6.4 all-to-all-start
  28.6 93.3 %all-to-all-done = f32[8,8,32768]{2,1,0:T(8,128)} async-done(((f32[8,8,32768]{2,1,0:T(8,128)}), f32[8,8,32768]{2,1,0:T(8,128)}, u32[]{:S(2)}, u32[]{:S(2)}) %all-to-all-start) | async-done | bytes 8388640 | tf_op jit(solution)/shard_map/all_to_all | solution.py:46
  121.9 23.5 %fusion.14 = f32[8,8,128,2,128]{4,3,2,1,0:T(2,128)} fusion(f32[8,8,128,2,128]{4,1,3,2,0:T(8,128)} %bitcast.3, s32[8,2]{1,0:T(8,128)S(1)} %gather_fusion), kind=kOutput, calls=%fused_computation.24 | convolution fusion | flops 50331680 | bytes 16777280 | tf_op jit(solution)/shard_map/stq,smitj->smiqj/dot_general | solution.py:61
  145.5 11.5 %reshape.254 = f32[64,32768]{1,0:T(8,128)} reshape(f32[8,8,128,2,128]{4,3,2,1,0:T(2,128)} %fusion.14) | data formatting | bytes 16777216 | tf_op jit(solution)/shard_map/reshape | solution.py:62
  157.0 10.1 %fusion.59 = f32[44,32768]{1,0:T(8,128)} fusion(f32[44,64]{0,1:T(8,128)S(1)} %convolution_bitcast_fusion, f32[64,32768]{1,0:T(8,128)} %reshape.254), kind=kOutput, calls=%fused_computation.138 | convolution fusion | flops 1107296256 | bytes 14167040 | tf_op jit(solution)/shard_map/dot_general | solution.py:63
  167.0 7.4 %reshape.255 = f32[5632,256]{1,0:T(8,128)} reshape(f32[44,32768]{1,0:T(8,128)} %fusion.59) | data formatting | bytes 11534336 | tf_op jit(solution)/shard_map/reshape | solution.py:63
  174.4 5.1 add.152
  179.5 4.5 slice_select_fusion
  184.0 1.5 copy-done
  185.5 174.4 %all-reduce.7.cloned.1.call-done = (f32[5632,128]{1,0:T(8,128)}, f32[5632,128]{1,0:T(8,128)}, f32[5632,128]{1,0:T(8,128)}, f32[5632,128]{1,0:T(8,128)}) async-done(((f32[5632,128]{1,0:T(8,128)}, f32[5632,128]{1,0:T(8,128)}, f32[5632,128]{1,0:T(8,128)}, f32[5632,128]{1,0:T(8,128)}), (f32[5632,128]{1,0:T(8,128)}, f32[5632,128]{1,0:T(8,128)}, f32[5632,128]{1,0:T(8,128)}, ...) | async-done | bytes 11534352 | tf_op jit(solution)/shard_map/psum | solution.py:12
  359.9 2.4 constant_dynamic-update-slice_fusion.3
  365.5 4.3 copy-done.3
  370.0 1.6 stack.2
  371.5 4.4 all-to-all-start.1
  376.1 24.6 %all-to-all-done.1 = f32[8,128,512]{1,2,0:T(8,128)S(1)} async-done(((f32[8,128,512]{1,2,0:T(8,128)}), f32[8,128,512]{1,2,0:T(8,128)S(1)}, u32[]{:S(2)}, u32[]{:S(2)}) %all-to-all-start.1) | async-done | bytes 2097184 | tf_op jit(solution)/shard_map/all_to_all | solution.py:74
  400.9 1.3 copy.39
  402.2 1.4 fusion.22
  404.2 11.7 %cholesky.104 = f32[128,128]{1,0:T(8,128)S(1)} custom-call(f32[128,128]{1,0:T(8,128)S(1)} %cholesky.266), custom_call_target="Cholesky" | custom-call | tf_op jit(solution)/shard_map/jit(cholesky)/cholesky | solution.py:76
  416.0 9.8 %custom-call.31 = f32[1,128,128]{1,2,0:T(8,128)S(1)} custom-call(f32[1,128,128]{2,1,0:T(8,128)S(1)} %get-tuple-element.44), custom_call_target="InvertDiagBlocksLowerTriangular" | custom-call | tf_op jit(solution)/shard_map/jit(cholesky)/cholesky | solution.py:76
  426.5 11.7 %cholesky.217 = f32[128,128]{1,0:T(8,128)S(1)} custom-call(f32[128,128]{1,0:T(8,128)S(1)} %cholesky.270), custom_call_target="Cholesky" | custom-call | tf_op jit(solution)/shard_map/jit(cholesky)/cholesky | solution.py:76
  438.3 10.0 %custom-call.32 = f32[1,128,128]{1,2,0:T(8,128)S(1)} custom-call(f32[1,128,128]{2,1,0:T(8,128)S(1)} %get-tuple-element.41), custom_call_target="InvertDiagBlocksLowerTriangular" | custom-call | tf_op jit(solution)/shard_map/jit(cholesky)/cholesky | solution.py:76
  448.9 11.7 %cholesky.238 = f32[128,128]{1,0:T(8,128)S(1)} custom-call(f32[128,128]{1,0:T(8,128)S(1)} %cholesky.275), custom_call_target="Cholesky" | custom-call | tf_op jit(solution)/shard_map/jit(cholesky)/cholesky | solution.py:76
  461.3 9.8 %custom-call.33 = f32[1,128,128]{1,2,0:T(8,128)S(1)} custom-call(f32[1,128,128]{2,1,0:T(8,128)S(1)} %get-tuple-element.38), custom_call_target="InvertDiagBlocksLowerTriangular" | custom-call | tf_op jit(solution)/shard_map/jit(cholesky)/cholesky | solution.py:76
  471.7 12.1 %cholesky.255 = f32[128,128]{1,0:T(8,128)S(1)} custom-call(f32[128,128]{1,0:T(8,128)S(1)} %convolution_subtract_fusion.5), custom_call_target="Cholesky" | custom-call | tf_op jit(solution)/shard_map/jit(cholesky)/cholesky | solution.py:76
  487.5 1.2 fusion.23
  488.7 7.2 while.1
  495.9 39.3 %custom-call.34 = f32[4,128,128]{1,2,0:T(8,128)S(1)} custom-call(f32[4,128,128]{2,1,0:T(8,128)S(1)} %get-tuple-element.12), custom_call_target="InvertDiagBlocksLowerTriangular" | custom-call | tf_op jit(solution)/shard_map/jit(_solve_triangular)/triangular_solve | solution.py:16
  535.2 4.4 fusion.19
  539.7 6.7 convolution_subtract_fusion.1
  546.4 2.8 fusion.35
  549.2 12.8 %convolution_subtract_fusion.2 = f32[128,5632]{0,1:T(8,128)S(1)} fusion(f32[128,5632]{1,0:T(8,128)S(1)} %fusion.35, f32[128,5632]{1,0:T(8,128)S(1)} %fusion.19, f32[512,5632]{0,1:T(8,128)} %bitcast.90, f32[512,512]{1,0:T(8,128)} %copy-done.6), kind=kOutput, calls=%fused_computation.18 | convolution fusion | flops 2216755200 | bytes 11665408 | tf_op jit(solution)/shard_map/jit(_solve_triangular)/triangular_solve | solution.py:16
  561.9 2.7 fusion.33
  564.7 1.6 copy-done.2
  566.3 17.4 %fusion.8 = f32[128,5632]{0,1:T(8,128)} fusion(f32[128,5632]{1,0:T(8,128)S(1)} %fusion.33, f32[128,5632]{1,0:T(8,128)S(1)} %fusion.35, f32[128,5632]{1,0:T(8,128)S(1)} %fusion.19, f32[512,5632]{0,1:T(8,128)} %bitcast.91, f32[512,512]{1,0:T(8,128)} %copy-done.6), kind=kOutput, calls=%fused_computation.19 | convolution fusion | flops 3326935040 | bytes 14614528 | tf_op jit(solution)/shard_map/jit(_solve_triangular)/triangular_solve | solution.py:16
  583.7 3.4 copy.46
  587.1 3.4 copy.45
  590.5 2.2 copy.44
  592.7 4.6 fusion.32
  597.3 6.0 maximum_bitcast_fusion
  603.3 9.7 %slice.165 = f32[5504,512]{1,0:T(8,128)} slice(f32[5632,512]{1,0:T(8,128)} %maximum_bitcast_fusion), slice={[128:5632], [0:512]} | slice | bytes 22544384 | tf_op jit(solution)/shard_map/slice | solution.py:82
  614.1 9.9 %pad_maximum_fusion = f32[5632,512]{1,0:T(8,128)} fusion(f32[128,512]{1,0:T(8,128)S(1)} %slice_select_fusion.4, f32[5504,512]{1,0:T(8,128)} %slice.165), kind=kLoop, calls=%fused_computation.5 | loop fusion | flops 2883584 | bytes 23068672 | tf_op jit(solution)/shard_map/concatenate | solution.py:82
  624.0 4.9 gather_fusion.1
  629.8 73.2 %all-reduce.5.cloned.1.call-done = f32[256,512]{1,0:T(8,128)} async-done(((f32[256,512]{1,0:T(8,128)}), f32[256,512]{1,0:T(8,128)}) %all-reduce.5.cloned.1.call-update) | async-done | bytes 524304 | tf_op jit(solution)/shard_map/psum | solution.py:12
  702.9 13.2 %convolution_subtract_fusion = f32[5632,256]{1,0:T(8,128)S(1)} fusion(f32[5632,256]{1,0:T(8,128)} %copy-done, f32[256,512]{1,0:T(8,128)} %all-reduce.5.cloned.1.call-done, f32[128,512]{1,0:T(8,128)S(1)} %slice_select_fusion.4, f32[5504,512]{1,0:T(8,128)} %slice.165), kind=kOutput, calls=%fused_computation.16 | convolution fusion | flops 8862695424 | bytes 23592960 | tf_op jit(solution)/shard_map/dot_general | solution.py:87
  716.2 2.6 fusion.18
  718.7 2.5 copy-done.12
  (85 shorter events, 19.4 us)
Async XLA Ops:
  21.0 6.7 copy-start.10
  21.0 100.9 %all-to-all-start = ((f32[8,8,32768]{2,1,0:T(8,128)}), f32[8,8,32768]{2,1,0:T(8,128)}, u32[]{:S(2)}, u32[]{:S(2)}) async-start(f32[8,8,32768]{2,1,0:T(8,128)} %fusion.42), calls=%async_computation | async-start | bytes 16777216 | tf_op jit(solution)/shard_map/all_to_all | solution.py:46
  27.4 332.4 %all-reduce.7.cloned.1.call-start = ((), (), s32[]{:S(2)}) async-start(), calls=%async_computation.3 | async-start | bytes 23068672 | tf_op jit(solution)/shard_map/psum | solution.py:12
  179.5 6.0 copy-start
  359.9 2.7 copy-start.9
  362.3 1.9 copy-start.8
  363.0 2.1 copy-start.7
  365.5 4.4 copy-start.3
  371.5 29.2 %all-to-all-start.1 = ((f32[8,128,512]{1,2,0:T(8,128)}), f32[8,128,512]{1,2,0:T(8,128)S(1)}, u32[]{:S(2)}, u32[]{:S(2)}) async-start(f32[8,128,512]{1,2,0:T(8,128)} %stack.2), calls=%async_computation.1 | async-start | bytes 4194304 | tf_op jit(solution)/shard_map/all_to_all | solution.py:74
  376.0 326.9 %all-reduce.5.cloned.1.call-start = ((), (), s32[]{:S(2)}) async-start(), calls=%async_computation.2 | async-start | bytes 1048576 | tf_op jit(solution)/shard_map/psum | solution.py:12
  495.9 39.3 %copy-start.6 = (f32[512,512]{1,0:T(8,128)}, f32[512,512]{1,0:T(8,128)S(1)}, u32[]{:S(2)}) copy-start(f32[512,512]{1,0:T(8,128)S(1)} %get-tuple-element.116) | copy-start | bytes 3145732
  549.1 15.5 %copy-start.1 = (f32[128,5632]{1,0:T(8,128)}, f32[128,5632]{1,0:T(8,128)S(1)}, u32[]{:S(2)}) copy-start(f32[128,5632]{1,0:T(8,128)S(1)} %fusion.35) | copy-start | bytes 8650756
  564.7 1.6 copy-start.2
  592.7 4.6 copy-start.4
  592.7 4.6 copy-start.5
  702.9 13.2 %copy-start.11 = (f32[5632,256]{1,0:T(8,128)S(1)}, f32[5632,256]{1,0:T(8,128)}, u32[]{:S(2)}) copy-start(f32[5632,256]{1,0:T(8,128)} %custom-call.42) | copy-start | bytes 17301508
  718.7 2.5 copy-start.12
Sparse Core Ops, SparseCore 0:
  185.6 174.1 all-reduce.6
  629.9 73.0 all-reduce.4
